TPU v7x, 32 devices: a whole 2x2x4 slice. The times are simulated.
32 devices in a mesh: alpha: 16 (over z, y, x), beta: 2 (over core).
Axes of the slice: x: 2, y: 2, z: 4, core: 2. Of those that a mesh axis runs over, the one named last changes fastest.
Arguments:
- coeffs: bfloat16 [1024, 512], P('alpha', 'beta'), may hold values from -6 to 6
- integrals: bfloat16 [484, 484], replicated, may hold values from -0.0234375 to 0.0234375
- send_block: int32 [16, 128], P('alpha'), may hold values from 0 to 16, as said below
- alpha_slot: int32 [256, 132], P('alpha'), may hold values from 0 to 63, as said below
- alpha_pair: int32 [256, 132], P('alpha'), may hold values from 0 to 483, as said below
- alpha_parity: int32 [256, 132], P('alpha'), may hold values from 0 to 1
- beta_pair: int32 [32, 132], P('beta'), may hold values from 0 to 483, as said below
- beta_target: int32 [32, 132], P('beta'), may hold values from 0 to 31
- beta_parity: int32 [32, 132], P('beta'), may hold values from 0 to 1
Outputs:
- sigma: float32 [1024, 512], P('alpha', 'beta')
Inputs may be any that keep to these rules, and one draw needn't show every extreme that they name: `send_block`: in each batch the filled slots from one sender to one receiver come first; at most 4 are filled, 4 is reached from every sender to some receiver in every batch, and some slots stay empty in every batch. `alpha_slot`: every entry names a slot that holds a block. `alpha_pair`: the pairs of one row are distinct. `beta_pair`: the pairs of one row are distinct.
All inputs are finite; a program needn't handle non-finite values.
Results may differ from a plain program's by a relative error of at most 0.0003.
Values may be sent and summed in bfloat16 or wider, within the bound.
No kernel may reach another device: no remote copies, remote signals or barrier semaphores. Data moves between devices by JAX's collectives and lax.ppermute only.
A program may use at most 64 MiB of HBM per device.

v0:
```python
import jax
import jax.numpy as jnp
from jax import lax
from jax.experimental import pallas as pl
from jax.experimental.pallas import tpu as pltpu
from jax.sharding import PartitionSpec as P

BATCHES = 2
CAP = 4
BF = jnp.bfloat16
F32 = jnp.float32
LANES = 128
WIDE = 256


def row_of(length):
    return lax.broadcasted_iota(jnp.int32, (1, length), 1)


def column_of(length):
    return lax.broadcasted_iota(jnp.int32, (length, 1), 0)


def over(x, n):
    if n & (n - 1) == 0:
        return lax.shift_right_logical(x, jnp.int32(n.bit_length() - 1))
    return lax.div(x, jnp.int32(n))


def modulo(x, n):
    if n & (n - 1) == 0:
        return x & (n - 1)
    return lax.rem(x, jnp.int32(n))


def one(condition):
    return jnp.where(condition, 1.0, 0.0).astype(BF)


def dot(a, b):
    return jnp.dot(a, b, preferred_element_type=F32)


def dot_nt(a, b):
    return lax.dot_general(a, b, (((1,), (1,)), ((), ())), preferred_element_type=F32)


def split(x):
    high = x.astype(BF)
    return high, (x - high.astype(F32)).astype(BF)


def outgoing_kernel(strings, width, coeffs_ref, send_ref, out_ref):
    rows, columns = coeffs_ref.shape
    slots = send_ref.shape[1]
    wide = strings * columns
    group = strings * width
    per = BATCHES * CAP
    n = row_of(wide)
    spread = one(column_of(columns) == over(n, group) * width + modulo(n, width))
    spaced = dot(coeffs_ref[...], spread)
    keep = modulo(column_of(rows), strings) == modulo(over(n, width), strings)
    spaced = jnp.where(keep, spaced, 0.0).astype(BF)
    r = column_of(slots)
    wanted = over(modulo(r, per), CAP) * (slots // BATCHES) + over(r, per) * CAP + modulo(r, CAP)
    chosen = jnp.sum(
        jnp.where(wanted == row_of(slots), send_ref[...].astype(F32), 0.0), axis=1, keepdims=True
    ).astype(jnp.int32)
    pick = one(over(row_of(rows), strings) == chosen)
    out_ref[...] = dot(pick, spaced).astype(BF)


def tables_kernel(beta_blocks, *refs):
    sources, target_ref, copies = refs[:7], refs[7], refs[8:15]
    out_ref, t_ref, w_ref, hot_ref, in_sems, out_sems = refs[15:]
    moves = [
        pltpu.make_async_copy(source, copy, in_sems.at[i])
        for i, (source, copy) in enumerate(zip(sources, copies))
    ]
    for move in moves:
        move.start()
    bpair_ref, btarget_ref, bparity_ref, slot_ref, pair_ref, parity_ref, integrals_ref = copies
    orbitals = integrals_ref.shape[0]
    blocks, excitations = slot_ref.shape
    beta_local, beta_excitations = bpair_ref.shape
    pairs = blocks // BATCHES
    slots = hot_ref.shape[0] // pairs
    for move in moves[:3]:
        move.wait()
    bpair = bpair_ref[...].astype(F32).T.astype(jnp.int32)
    bfactor = (1 - 2 * bparity_ref[...]).astype(F32)
    btarget = btarget_ref[...] - lax.axis_index("beta") * beta_local
    btarget = jnp.where(btarget < 0, btarget + beta_blocks, btarget)
    for v in range(beta_local):
        left = jnp.where(column_of(beta_blocks) == btarget[v : v + 1], bfactor[v : v + 1], 0.0)
        right = one(row_of(orbitals) == bpair[:, v : v + 1])
        t_ref[v * beta_blocks : (v + 1) * beta_blocks, :] = dot(left.astype(BF), right).astype(BF)
    for move in moves[3:]:
        move.wait()
    high, low = split(dot(t_ref[...], integrals_ref[...]))
    w_ref[0] = high
    w_ref[1] = low
    pair = pair_ref[...].astype(F32).T.astype(jnp.int32)
    factor = (1 - 2 * parity_ref[...]).astype(F32)
    slot = slot_ref[...]
    place = over(slot, CAP) * (BATCHES * CAP) + modulo(slot, CAP)
    for t in range(pairs):
        total = None
        for h in range(BATCHES):
            g = h * pairs + t
            row = place[g : g + 1] + h * CAP
            left = jnp.where(column_of(slots) == row, factor[g : g + 1], 0.0).astype(BF)
            part = dot(left, one(row_of(orbitals) == pair[:, g : g + 1]))
            total = part if total is None else total + part
        hot_ref[t * slots : (t + 1) * slots, :] = total.astype(BF)
    step = max(1, WIDE // slots)
    results = []
    for start in range(0, pairs, step):
        hot = hot_ref[start * slots : (start + step) * slots, :]
        high, low = split(dot_nt(w_ref[0], hot) + dot_nt(w_ref[1], hot))
        for i in range(step):
            rows = slice((start + i) * beta_blocks, (start + i + 1) * beta_blocks)
            lanes = slice(i * slots, (i + 1) * slots)
            for v in range(beta_local):
                source = slice(v * beta_blocks, (v + 1) * beta_blocks)
                first = v * 2 * slots
                out_ref[rows, first : first + slots] = high[source, lanes]
                out_ref[rows, first + slots : first + 2 * slots] = low[source, lanes]
        done = pl.ds(start * beta_blocks, step * beta_blocks)
        result = pltpu.make_async_copy(out_ref.at[done], target_ref.at[done], out_sems.at[start])
        result.start()
        results.append(result)
    for result in results:
        result.wait()


def sigma_kernel(strings, width, table_ref, received_ref, *refs):
    outs, (right_ref, sum_ref, place_ref) = refs[:-3], refs[-3:]
    slots, wide = received_ref.shape
    group = strings * width
    both = BATCHES * group
    pairs = outs[0].shape[0] // strings // BATCHES
    blocks = table_ref.shape[0] // pairs
    batch = modulo(over(column_of(slots), CAP), BATCHES)
    low = one((batch == 0) & (row_of(both) < group))
    high = one((batch == 1) & (row_of(both) >= group))
    for tile in range(wide // both):
        x = received_ref[:, tile * both : (tile + 1) * both]
        turned = jnp.concatenate([x[:, group:], x[:, :group]], axis=1)
        for v, (a, b) in ((2 * tile, (x, turned)), (2 * tile + 1, (turned, x))):
            value = a * low + b * high
            right_ref[2 * v * slots : (2 * v + 1) * slots, :] = value
            right_ref[(2 * v + 1) * slots : (2 * v + 2) * slots, :] = value
    product = dot(table_ref[...], right_ref[...])
    both_parts = jnp.concatenate(split(product), axis=1)
    per_tile = LANES // width
    columns = BATCHES * strings * LANES
    n = row_of(columns)
    expand = one(
        modulo(column_of(2 * both), both) == over(n, LANES) * width + modulo(n, width)
    )
    spread = dot(both_parts, expand)
    keep = modulo(column_of(pairs * blocks), per_tile) == modulo(over(n, width), per_tile)
    spread = jnp.where(keep, spread, 0.0)
    tiles = blocks // per_tile
    summed = jnp.sum(spread.reshape(pairs * tiles, per_tile, columns), axis=1)
    for hs in range(BATCHES * strings):
        sum_ref[hs] = summed[:, hs * LANES : (hs + 1) * LANES]
    per_out = tiles // len(outs)
    for q in range(tiles):
        for h in range(BATCHES):
            for s in range(strings):
                place_ref[q, pl.ds(h * pairs * strings + s, pairs, stride=strings), :] = sum_ref[
                    h * strings + s, pl.ds(q, pairs, stride=tiles), :
                ]
        at = q % per_out * LANES
        outs[q // per_out][:, at : at + LANES] = place_ref[q]


def on_device(
    coeffs,
    integrals,
    send_block,
    alpha_slot,
    alpha_pair,
    alpha_parity,
    beta_pair,
    beta_target,
    beta_parity,
):
    local_rows, local_columns = coeffs.shape
    local_blocks = alpha_slot.shape[0]
    strings = local_rows // local_blocks
    pairs = local_blocks // BATCHES
    beta_local = beta_pair.shape[0]
    width = local_columns // beta_local
    cores = lax.axis_size("beta")
    senders = lax.axis_size("alpha")
    beta_blocks = cores * beta_local
    orbitals = integrals.shape[0]
    slots = send_block.shape[1]
    wide = strings * local_columns

    outgoing = pl.pallas_call(
        lambda *refs: outgoing_kernel(strings, width, *refs),
        out_shape=jax.ShapeDtypeStruct((slots, wide), BF),
        compiler_params=pltpu.CompilerParams(vmem_limit_bytes=60 * 2**20),
        name="outgoing",
    )(coeffs, send_block)
    received = lax.all_to_all(
        outgoing.reshape(senders, slots // senders, wide), "alpha", split_axis=0, concat_axis=0, tiled=True
    ).reshape(slots, wide)
    tables = (
        beta_pair,
        beta_target,
        beta_parity,
        alpha_slot,
        alpha_pair,
        alpha_parity,
        integrals,
    )
    flops = 2 * beta_local * beta_blocks * orbitals * (orbitals + 2 * pairs * slots)
    shape = (pairs * beta_blocks, 2 * beta_local * slots)
    table = pl.pallas_call(
        lambda *refs: tables_kernel(beta_blocks, *refs),
        in_specs=[pl.BlockSpec(memory_space=pltpu.HBM)] * len(tables),
        out_specs=pl.BlockSpec(memory_space=pltpu.HBM),
        out_shape=jax.ShapeDtypeStruct(shape, BF),
        scratch_shapes=[pltpu.VMEM(x.shape, x.dtype) for x in tables]
        + [
            pltpu.VMEM(shape, BF),
            pltpu.VMEM((beta_local * beta_blocks, orbitals), BF),
            pltpu.VMEM((2, beta_local * beta_blocks, orbitals), BF),
            pltpu.VMEM((pairs * slots, orbitals), BF),
            pltpu.SemaphoreType.DMA((len(tables),)),
            pltpu.SemaphoreType.DMA((pairs,)),
        ],
        compiler_params=pltpu.CompilerParams(vmem_limit_bytes=60 * 2**20),
        cost_estimate=pl.CostEstimate(flops=flops, bytes_accessed=8 * 2**20, transcendentals=0),
        name="tables",
    )(*tables)
    part = jax.ShapeDtypeStruct((local_rows, local_columns), F32)
    both = BATCHES * strings * width
    tiles = beta_blocks * width // LANES
    parts = pl.pallas_call(
        lambda *refs: sigma_kernel(strings, width, *refs),
        out_shape=[part] * cores,
        scratch_shapes=[
            pltpu.VMEM((2 * beta_local * slots, both), BF),
            pltpu.VMEM((BATCHES * strings, pairs * tiles, LANES), F32),
            pltpu.VMEM((tiles, local_rows, LANES), F32),
        ],
        compiler_params=pltpu.CompilerParams(vmem_limit_bytes=40 * 2**20),
        name="sigma",
    )(table, received)
    result = parts[0]
    for step in range(1, cores):
        route = [(core, (core + step) % cores) for core in range(cores)]
        result = result + lax.ppermute(parts[step], "beta", route)
    return result


def solution(mesh):
    in_specs = (
        P("alpha", "beta"),
        P(),
        P("alpha", None),
        P("alpha", None),
        P("alpha", None),
        P("alpha", None),
        P("beta", None),
        P("beta", None),
        P("beta", None),
    )
    out_specs = P("alpha", "beta")
    return jax.shard_map(
        on_device, mesh=mesh, in_specs=in_specs, out_specs=out_specs, check_vma=False
    )
```

profile of v0, /device:TPU:0, one launch (start us, length us, event | category | flops | bytes accessed | tf_op | source)
XLA Modules:
  0.0 24.8 jit_solution(5686085289730056754)
XLA Ops:
  0.0 1.9 %outgoing.1 = bf16[128,1024]{1,0:T(8,128)(2,1)} custom-call(bf16[64,256]{1,0:T(8,128)(2,1)} %refs_0_.3, s32[1,128]{1,0:T(1,128)} %refs_1_.3), custom_call_target="tpu_custom_call" | custom-call | tf_op jit(solution)/shard_map/outgoing/pallas_call | solution.py:204
  1.9 8.3 %all-to-all-start = ((bf16[16,8,1024]{2,1,0:T(8,128)(2,1)}), bf16[16,8,1024]{2,1,0:T(8,128)(2,1)S(1)}, u32[]{:S(2)}, u32[]{:S(2)}) async-start(bf16[16,8,1024]{2,1,0:T(8,128)(2,1)} %bitcast.3), calls=%async_computation | async-start | bytes 524288 | tf_op jit(solution)/shard_map/all_to_all | solution.py:210
  10.2 5.0 %tables.1.refs_0_ = bf16[256,4096]{1,0:T(8,128)(2,1)} custom-call(s32[16,132]{1,0:T(8,128)} %refs_0_.2, s32[16,132]{1,0:T(8,128)} %refs_1_.2, s32[16,132]{1,0:T(8,128)} %refs_2_.1, s32[16,132]{1,0:T(8,128)} %refs_3_.1, s32[16,132]{1,0:T(8,128)} %refs_4_.1, s32[16,132]{1,0:T(8,128)} %refs_5_.1, bf16[484,484]{1,0:T(8,128)(2,1)} %refs_6_.1), custom_call_target="tpu_custom_call" | custom-call | flops 1254899712 | bytes 8388608 | tf_op jit(solution)/shard_map/tables/pallas_call | solution.py:224
  15.2 4.8 %all-to-all-done = bf16[16,8,1024]{2,1,0:T(8,128)(2,1)S(1)} async-done(((bf16[16,8,1024]{2,1,0:T(8,128)(2,1)}), bf16[16,8,1024]{2,1,0:T(8,128)(2,1)S(1)}, u32[]{:S(2)}, u32[]{:S(2)}) %all-to-all-start) | async-done | bytes 262176 | tf_op jit(solution)/shard_map/all_to_all | solution.py:210
  20.1 0.0 copy-start
  20.1 1.6 %copy-done = bf16[256,4096]{1,0:T(8,128)(2,1)S(1)} copy-done((bf16[256,4096]{1,0:T(8,128)(2,1)S(1)}, bf16[256,4096]{1,0:T(8,128)(2,1)}, u32[]{:S(2)}) %copy-start) | copy-done | bytes 2097176
  21.7 1.2 %sigma.1 = (f32[64,256]{1,0:T(8,128)S(1)}, f32[64,256]{1,0:T(8,128)S(1)}) custom-call(bf16[256,4096]{1,0:T(8,128)(2,1)S(1)} %copy-done, bf16[128,1024]{1,0:T(8,128)(2,1)S(1)} %bitcast.2), custom_call_target="tpu_custom_call" | custom-call | tf_op jit(solution)/shard_map/sigma/pallas_call | solution.py:245
  22.9 0.1 collective-permute-start
  22.9 1.2 %collective-permute-done = f32[64,256]{1,0:T(8,128)S(1)} collective-permute-done((f32[64,256]{1,0:T(8,128)S(1)}, f32[64,256]{1,0:T(8,128)S(1)}, u32[]{:S(2)}, u32[]{:S(2)}) %collective-permute-start) | collective-permute-done | bytes 65568 | tf_op jit(solution)/shard_map/ppermute | solution.py:259
  24.2 0.6 %add.3 = f32[64,256]{1,0:T(8,128)} add(f32[64,256]{1,0:T(8,128)S(1)} %get-tuple-element.7, f32[64,256]{1,0:T(8,128)S(1)} %collective-permute-done) | non-fusion elementwise | flops 16384 | bytes 196608 | tf_op jit(solution)/shard_map/add | solution.py:259
Async XLA Ops:
  1.9 18.2 %all-to-all-start = ((bf16[16,8,1024]{2,1,0:T(8,128)(2,1)}), bf16[16,8,1024]{2,1,0:T(8,128)(2,1)S(1)}, u32[]{:S(2)}, u32[]{:S(2)}) async-start(bf16[16,8,1024]{2,1,0:T(8,128)(2,1)} %bitcast.3), calls=%async_computation | async-start | bytes 524288 | tf_op jit(solution)/shard_map/all_to_all | solution.py:210
  20.1 1.6 %copy-start = (bf16[256,4096]{1,0:T(8,128)(2,1)S(1)}, bf16[256,4096]{1,0:T(8,128)(2,1)}, u32[]{:S(2)}) copy-start(bf16[256,4096]{1,0:T(8,128)(2,1)} %tables.1.refs_0_) | copy-start | bytes 6291460
  22.9 1.3 %collective-permute-start = (f32[64,256]{1,0:T(8,128)S(1)}, f32[64,256]{1,0:T(8,128)S(1)}, u32[]{:S(2)}, u32[]{:S(2)}) collective-permute-start(f32[64,256]{1,0:T(8,128)S(1)} %get-tuple-element.8), channel_id=1, source_target_pairs={{0,1},{1,0},{2,3},{3,2},{4,5},{5,4},{6,7},{7,6},{8,9},{9,8},{10,11... | collective-permute-start | bytes 196616 | tf_op jit(solution)/shard_map/ppermute | solution.py:259
where the time goes:
time: 25.2 us; the launch traced here: 24.8 us
  starting transfers between devices  8.38 us (33%)
  Pallas kernels  8.11 us (32%)
  waiting for transfers between devices  6.07 us (24%)
  local copies, waits for them, and re-layouts  1.59 us (6%)
  other arithmetic  0.64 us (3%)
    all_to_all x1, starting transfers between devices, on_device(): lax.all_to_all(outgoing.reshape(senders, slots // senders, wide), 'alpha'...  8.31 us
    pallas_call x1, Pallas kernels, on_device(): pl.pallas_call(lambda *refs: tables_kernel(beta_blocks, *refs), in_specs=...  5.03 us
    all_to_all x1, waiting for transfers between devices, on_device(): lax.all_to_all(outgoing.reshape(senders, slots // senders, wide), 'alpha'...  4.83 us
    pallas_call x1, Pallas kernels, on_device(): pl.pallas_call(lambda *refs: outgoing_kernel(strings, width, *refs), out_...  1.88 us
    unnamed x2, local copies, waits for them, and re-layouts  1.59 us
    ppermute x1, waiting for transfers between devices, on_device(): result = result + lax.ppermute(parts[step], 'beta', route)  1.24 us
    pallas_call x1, Pallas kernels, on_device(): pl.pallas_call(lambda *refs: sigma_kernel(strings, width, *refs), out_sha...  1.2 us
    add x1, other arithmetic, on_device(): result = result + lax.ppermute(parts[step], 'beta', route)  0.64 us
  transfers between devices with their start and end apart: 2, of which 2 were waited for; matrix products, arithmetic and copies ran while one was open for 0% of the time, Pallas kernels for 20%

commit v1 on v0

--- a/solution.py
+++ b/solution.py
@@ -50,7 +50,16 @@
     return high, (x - high.astype(F32)).astype(BF)
 
 
-def outgoing_kernel(strings, width, coeffs_ref, send_ref, out_ref):
+def outgoing_kernel(strings, width, *refs):
+    count = (len(refs) - 6) // 2
+    sources, out_ref, copies = refs[: 2 + count], refs[2 + count], refs[3 + count : -3]
+    coeffs_ref, send_ref, sems = refs[-3:]
+    moves = [
+        pltpu.make_async_copy(source, target, sems.at[i])
+        for i, (source, target) in enumerate(zip(sources, (coeffs_ref, send_ref, *copies)))
+    ]
+    for move in moves:
+        move.start()
     rows, columns = coeffs_ref.shape
     slots = send_ref.shape[1]
     wide = strings * columns
@@ -58,35 +67,40 @@
     per = BATCHES * CAP
     n = row_of(wide)
     spread = one(column_of(columns) == over(n, group) * width + modulo(n, width))
-    spaced = dot(coeffs_ref[...], spread)
     keep = modulo(column_of(rows), strings) == modulo(over(n, width), strings)
-    spaced = jnp.where(keep, spaced, 0.0).astype(BF)
     r = column_of(slots)
     wanted = over(modulo(r, per), CAP) * (slots // BATCHES) + over(r, per) * CAP + modulo(r, CAP)
+    moves[0].wait()
+    moves[1].wait()
+    spaced = jnp.where(keep, dot(coeffs_ref[...], spread), 0.0).astype(BF)
     chosen = jnp.sum(
         jnp.where(wanted == row_of(slots), send_ref[...].astype(F32), 0.0), axis=1, keepdims=True
     ).astype(jnp.int32)
     pick = one(over(row_of(rows), strings) == chosen)
     out_ref[...] = dot(pick, spaced).astype(BF)
-
-
-def tables_kernel(beta_blocks, *refs):
-    sources, target_ref, copies = refs[:7], refs[7], refs[8:15]
-    out_ref, t_ref, w_ref, hot_ref, in_sems, out_sems = refs[15:]
-    moves = [
-        pltpu.make_async_copy(source, copy, in_sems.at[i])
-        for i, (source, copy) in enumerate(zip(sources, copies))
-    ]
-    for move in moves:
-        move.start()
-    bpair_ref, btarget_ref, bparity_ref, slot_ref, pair_ref, parity_ref, integrals_ref = copies
+    for move in moves[2:]:
+        move.wait()
+
+
+def tables_kernel(
+    beta_blocks,
+    slot_ref,
+    pair_ref,
+    parity_ref,
+    bpair_ref,
+    btarget_ref,
+    bparity_ref,
+    integrals_ref,
+    out_ref,
+    t_ref,
+    w_ref,
+    hot_ref,
+):
     orbitals = integrals_ref.shape[0]
     blocks, excitations = slot_ref.shape
     beta_local, beta_excitations = bpair_ref.shape
     pairs = blocks // BATCHES
     slots = hot_ref.shape[0] // pairs
-    for move in moves[:3]:
-        move.wait()
     bpair = bpair_ref[...].astype(F32).T.astype(jnp.int32)
     bfactor = (1 - 2 * bparity_ref[...]).astype(F32)
     btarget = btarget_ref[...] - lax.axis_index("beta") * beta_local
@@ -95,8 +109,6 @@
         left = jnp.where(column_of(beta_blocks) == btarget[v : v + 1], bfactor[v : v + 1], 0.0)
         right = one(row_of(orbitals) == bpair[:, v : v + 1])
         t_ref[v * beta_blocks : (v + 1) * beta_blocks, :] = dot(left.astype(BF), right).astype(BF)
-    for move in moves[3:]:
-        move.wait()
     high, low = split(dot(t_ref[...], integrals_ref[...]))
     w_ref[0] = high
     w_ref[1] = low
@@ -114,7 +126,6 @@
             total = part if total is None else total + part
         hot_ref[t * slots : (t + 1) * slots, :] = total.astype(BF)
     step = max(1, WIDE // slots)
-    results = []
     for start in range(0, pairs, step):
         hot = hot_ref[start * slots : (start + step) * slots, :]
         high, low = split(dot_nt(w_ref[0], hot) + dot_nt(w_ref[1], hot))
@@ -126,12 +137,6 @@
                 first = v * 2 * slots
                 out_ref[rows, first : first + slots] = high[source, lanes]
                 out_ref[rows, first + slots : first + 2 * slots] = low[source, lanes]
-        done = pl.ds(start * beta_blocks, step * beta_blocks)
-        result = pltpu.make_async_copy(out_ref.at[done], target_ref.at[done], out_sems.at[start])
-        result.start()
-        results.append(result)
-    for result in results:
-        result.wait()
 
 
 def sigma_kernel(strings, width, table_ref, received_ref, *refs):
@@ -201,41 +206,41 @@
     slots = send_block.shape[1]
     wide = strings * local_columns
 
-    outgoing = pl.pallas_call(
+    others = (
+        alpha_slot,
+        alpha_pair,
+        alpha_parity,
+        beta_pair,
+        beta_target,
+        beta_parity,
+        integrals,
+    )
+    outgoing, *tables = pl.pallas_call(
         lambda *refs: outgoing_kernel(strings, width, *refs),
-        out_shape=jax.ShapeDtypeStruct((slots, wide), BF),
-        compiler_params=pltpu.CompilerParams(vmem_limit_bytes=60 * 2**20),
+        in_specs=[pl.BlockSpec(memory_space=pltpu.HBM)] * (2 + len(others)),
+        out_shape=[jax.ShapeDtypeStruct((slots, wide), BF)]
+        + [jax.ShapeDtypeStruct(x.shape, x.dtype) for x in others],
+        scratch_shapes=[
+            pltpu.VMEM(coeffs.shape, BF),
+            pltpu.VMEM(send_block.shape, jnp.int32),
+            pltpu.SemaphoreType.DMA((2 + len(others),)),
+        ],
+        compiler_params=pltpu.CompilerParams(vmem_limit_bytes=40 * 2**20),
         name="outgoing",
-    )(coeffs, send_block)
+    )(*(pltpu.with_memory_space_constraint(x, pltpu.HBM) for x in (coeffs, send_block, *others)))
     received = lax.all_to_all(
         outgoing.reshape(senders, slots // senders, wide), "alpha", split_axis=0, concat_axis=0, tiled=True
     ).reshape(slots, wide)
-    tables = (
-        beta_pair,
-        beta_target,
-        beta_parity,
-        alpha_slot,
-        alpha_pair,
-        alpha_parity,
-        integrals,
-    )
     flops = 2 * beta_local * beta_blocks * orbitals * (orbitals + 2 * pairs * slots)
-    shape = (pairs * beta_blocks, 2 * beta_local * slots)
     table = pl.pallas_call(
         lambda *refs: tables_kernel(beta_blocks, *refs),
-        in_specs=[pl.BlockSpec(memory_space=pltpu.HBM)] * len(tables),
-        out_specs=pl.BlockSpec(memory_space=pltpu.HBM),
-        out_shape=jax.ShapeDtypeStruct(shape, BF),
-        scratch_shapes=[pltpu.VMEM(x.shape, x.dtype) for x in tables]
-        + [
-            pltpu.VMEM(shape, BF),
+        out_shape=jax.ShapeDtypeStruct((pairs * beta_blocks, 2 * beta_local * slots), BF),
+        scratch_shapes=[
             pltpu.VMEM((beta_local * beta_blocks, orbitals), BF),
             pltpu.VMEM((2, beta_local * beta_blocks, orbitals), BF),
             pltpu.VMEM((pairs * slots, orbitals), BF),
-            pltpu.SemaphoreType.DMA((len(tables),)),
-            pltpu.SemaphoreType.DMA((pairs,)),
         ],
-        compiler_params=pltpu.CompilerParams(vmem_limit_bytes=60 * 2**20),
+        compiler_params=pltpu.CompilerParams(vmem_limit_bytes=40 * 2**20),
         cost_estimate=pl.CostEstimate(flops=flops, bytes_accessed=8 * 2**20, transcendentals=0),
         name="tables",
     )(*tables)

time: 25.2 us -> 23.6 us (0.937)
  waiting for transfers between devices: 6.07 us -> 8.08 us
  Pallas kernels: 8.11 us -> 6.17 us
  local copies, waits for them, and re-layouts: 1.59 us -> 0 us
    all_to_all x1, waiting for transfers between devices: 4.83 us -> 6.84 us  [on_device(): lax.all_to_all(outgoing.reshape(senders, slots // senders, wide), 'alpha'...]
    pallas_call x2, Pallas kernels: 6.91 us -> 4.96 us  [the longest x1 3.02 us: on_device(): pl.pallas_call(lambda *refs: tables_kernel(beta_blocks, *refs), out_shape...]
    unnamed x2 -> x0, local copies, waits for them, and re-layouts: 1.59 us -> none
  transfers between devices with their start and end apart: 2 -> 2, of which waited for: 2 -> 2; matrix products, arithmetic and copies ran while one was open for 0% -> 0% of each run, Pallas kernels for 20% -> 13%
where the time goes in v1:
time: 23.6 us; the launch traced here: 23.3 us
  starting transfers between devices  8.4 us (36%)
  waiting for transfers between devices  8.08 us (34%)
  Pallas kernels  6.17 us (26%)
  other arithmetic  0.64 us (3%)
    all_to_all x1, starting transfers between devices, on_device(): lax.all_to_all(outgoing.reshape(senders, slots // senders, wide), 'alpha'...  8.32 us
    all_to_all x1, waiting for transfers between devices, on_device(): lax.all_to_all(outgoing.reshape(senders, slots // senders, wide), 'alpha'...  6.84 us
    pallas_call x1, Pallas kernels, on_device(): pl.pallas_call(lambda *refs: tables_kernel(beta_blocks, *refs), out_shape...  3.02 us
    pallas_call x1, Pallas kernels, on_device(): pl.pallas_call(lambda *refs: outgoing_kernel(strings, width, *refs), in_s...  1.94 us
    ppermute x1, waiting for transfers between devices, on_device(): result = result + lax.ppermute(parts[step], 'beta', route)  1.24 us
    pallas_call x1, Pallas kernels, on_device(): pl.pallas_call(lambda *refs: sigma_kernel(strings, width, *refs), out_sha...  1.2 us
    add x1, other arithmetic, on_device(): result = result + lax.ppermute(parts[step], 'beta', route)  0.64 us
  transfers between devices with their start and end apart: 2, of which 2 were waited for; matrix products, arithmetic and copies ran while one was open for 0% of the time, Pallas kernels for 13%

profile of v1, /device:TPU:0, one launch (start us, length us, event | category | flops | bytes accessed | tf_op | source)
XLA Modules:
  0.0 23.3 jit_solution(1546606104190671174)
XLA Ops:
  0.0 1.9 %outgoing.1 = (bf16[128,1024]{1,0:T(8,128)(2,1)}, s32[16,132]{1,0:T(8,128)S(1)}, s32[16,132]{1,0:T(8,128)S(1)}, s32[16,132]{1,0:T(8,128)S(1)}, s32[16,132]{1,0:T...) custom-call(bf16[64,256]{1,0:T(8,128)(2,1)} %refs_0_.1, ...), custom_call_target="tpu_custom_call" | custom-call | tf_op jit(solution)/shard_map/outgoing/pallas_call | solution.py:218
  2.0 8.3 %all-to-all-start = ((bf16[16,8,1024]{2,1,0:T(8,128)(2,1)}), bf16[16,8,1024]{2,1,0:T(8,128)(2,1)S(1)}, u32[]{:S(2)}, u32[]{:S(2)}) async-start(bf16[16,8,1024]{2,1,0:T(8,128)(2,1)} %bitcast), calls=%async_computation | async-start | bytes 524288 | tf_op jit(solution)/shard_map/all_to_all | solution.py:231
  10.3 3.0 %tables.1.refs_0_ = bf16[256,4096]{1,0:T(8,128)(2,1)S(1)} custom-call(s32[16,132]{1,0:T(8,128)S(1)} %get-tuple-element.15.refs_0_, s32[16,132]{1,0:T(8,128)S(1)} %get-tuple-element.16.refs_1_, s32[16,132]{1,0:T(8,128)S(1)} %get-tuple-element.17.refs_2_, s32[16,132]{1,0:T(8,128)S(1)} %get-tuple-element.18.refs_3_, s32[16,132]{1,0:T(8,128)S(1)} %get-tuple-element.19.refs_4_, ...), custom_call_target="tpu_custom_call" | custom-call | flops 1254899712 | bytes 8388608 | tf_op jit(solution)/shard_map/tables/pallas_call | solution.py:235
  13.3 6.8 %all-to-all-done = bf16[16,8,1024]{2,1,0:T(8,128)(2,1)S(1)} async-done(((bf16[16,8,1024]{2,1,0:T(8,128)(2,1)}), bf16[16,8,1024]{2,1,0:T(8,128)(2,1)S(1)}, u32[]{:S(2)}, u32[]{:S(2)}) %all-to-all-start) | async-done | bytes 262176 | tf_op jit(solution)/shard_map/all_to_all | solution.py:231
  20.2 1.2 %sigma.1 = (f32[64,256]{1,0:T(8,128)S(1)}, f32[64,256]{1,0:T(8,128)S(1)}) custom-call(bf16[256,4096]{1,0:T(8,128)(2,1)S(1)} %tables.1.refs_0_, bf16[128,1024]{1,0:T(8,128)(2,1)S(1)} %bitcast.2), custom_call_target="tpu_custom_call" | custom-call | tf_op jit(solution)/shard_map/sigma/pallas_call | solution.py:250
  21.4 0.1 collective-permute-start
  21.4 1.2 %collective-permute-done = f32[64,256]{1,0:T(8,128)S(1)} collective-permute-done((f32[64,256]{1,0:T(8,128)S(1)}, f32[64,256]{1,0:T(8,128)S(1)}, u32[]{:S(2)}, u32[]{:S(2)}) %collective-permute-start) | collective-permute-done | bytes 65568 | tf_op jit(solution)/shard_map/ppermute | solution.py:264
  22.7 0.6 %add.3 = f32[64,256]{1,0:T(8,128)} add(f32[64,256]{1,0:T(8,128)S(1)} %get-tuple-element.23, f32[64,256]{1,0:T(8,128)S(1)} %collective-permute-done) | non-fusion elementwise | flops 16384 | bytes 196608 | tf_op jit(solution)/shard_map/add | solution.py:264
Async XLA Ops:
  2.0 18.2 %all-to-all-start = ((bf16[16,8,1024]{2,1,0:T(8,128)(2,1)}), bf16[16,8,1024]{2,1,0:T(8,128)(2,1)S(1)}, u32[]{:S(2)}, u32[]{:S(2)}) async-start(bf16[16,8,1024]{2,1,0:T(8,128)(2,1)} %bitcast), calls=%async_computation | async-start | bytes 524288 | tf_op jit(solution)/shard_map/all_to_all | solution.py:231
  21.4 1.3 %collective-permute-start = (f32[64,256]{1,0:T(8,128)S(1)}, f32[64,256]{1,0:T(8,128)S(1)}, u32[]{:S(2)}, u32[]{:S(2)}) collective-permute-start(f32[64,256]{1,0:T(8,128)S(1)} %get-tuple-element.24), channel_id=1, source_target_pairs={{0,1},{1,0},{2,3},{3,2},{4,5},{5,4},{6,7},{7,6},{8,9},{9,8},{10,11... | collective-permute-start | bytes 196616 | tf_op jit(solution)/shard_map/ppermute | solution.py:264

commit v2 on v1

--- a/solution.py
+++ b/solution.py
@@ -50,7 +50,7 @@
     return high, (x - high.astype(F32)).astype(BF)
 
 
-def outgoing_kernel(strings, width, *refs):
+def outgoing_kernel(strings, width, outer, inner, *refs):
     count = (len(refs) - 6) // 2
     sources, out_ref, copies = refs[: 2 + count], refs[2 + count], refs[3 + count : -3]
     coeffs_ref, send_ref, sems = refs[-3:]
@@ -69,7 +69,8 @@
     spread = one(column_of(columns) == over(n, group) * width + modulo(n, width))
     keep = modulo(column_of(rows), strings) == modulo(over(n, width), strings)
     r = column_of(slots)
-    wanted = over(modulo(r, per), CAP) * (slots // BATCHES) + over(r, per) * CAP + modulo(r, CAP)
+    receiver = modulo(over(r, per), outer) * inner + over(over(r, per), outer)
+    wanted = over(modulo(r, per), CAP) * (slots // BATCHES) + receiver * CAP + modulo(r, CAP)
     moves[0].wait()
     moves[1].wait()
     spaced = jnp.where(keep, dot(coeffs_ref[...], spread), 0.0).astype(BF)
@@ -84,6 +85,8 @@
 
 def tables_kernel(
     beta_blocks,
+    outer,
+    inner,
     slot_ref,
     pair_ref,
     parity_ref,
@@ -115,7 +118,9 @@
     pair = pair_ref[...].astype(F32).T.astype(jnp.int32)
     factor = (1 - 2 * parity_ref[...]).astype(F32)
     slot = slot_ref[...]
-    place = over(slot, CAP) * (BATCHES * CAP) + modulo(slot, CAP)
+    sender = over(slot, CAP)
+    place = modulo(sender, inner) * outer + over(sender, inner)
+    place = place * (BATCHES * CAP) + modulo(slot, CAP)
     for t in range(pairs):
         total = None
         for h in range(BATCHES):
@@ -206,6 +211,9 @@
     slots = send_block.shape[1]
     wide = strings * local_columns
 
+    outer = 1 << (senders.bit_length() - 1) // 2
+    inner = senders // outer
+    order = [k * inner + i for i in range(inner) for k in range(outer)]
     others = (
         alpha_slot,
         alpha_pair,
@@ -216,7 +224,7 @@
         integrals,
     )
     outgoing, *tables = pl.pallas_call(
-        lambda *refs: outgoing_kernel(strings, width, *refs),
+        lambda *refs: outgoing_kernel(strings, width, outer, inner, *refs),
         in_specs=[pl.BlockSpec(memory_space=pltpu.HBM)] * (2 + len(others)),
         out_shape=[jax.ShapeDtypeStruct((slots, wide), BF)]
         + [jax.ShapeDtypeStruct(x.shape, x.dtype) for x in others],
@@ -229,11 +237,16 @@
         name="outgoing",
     )(*(pltpu.with_memory_space_constraint(x, pltpu.HBM) for x in (coeffs, send_block, *others)))
     received = lax.all_to_all(
-        outgoing.reshape(senders, slots // senders, wide), "alpha", split_axis=0, concat_axis=0, tiled=True
+        outgoing.reshape(senders, slots // senders, wide),
+        "alpha",
+        split_axis=0,
+        concat_axis=0,
+        axis_index_groups=[order],
+        tiled=True,
     ).reshape(slots, wide)
     flops = 2 * beta_local * beta_blocks * orbitals * (orbitals + 2 * pairs * slots)
     table = pl.pallas_call(
-        lambda *refs: tables_kernel(beta_blocks, *refs),
+        lambda *refs: tables_kernel(beta_blocks, outer, inner, *refs),
         out_shape=jax.ShapeDtypeStruct((pairs * beta_blocks, 2 * beta_local * slots), BF),
         scratch_shapes=[
             pltpu.VMEM((beta_local * beta_blocks, orbitals), BF),

time: 23.6 us -> 24.3 us (1.030)
  waiting for transfers between devices: 8.08 us -> 8.78 us
    all_to_all x1, waiting for transfers between devices: 6.84 us -> 7.53 us  [on_device(): lax.all_to_all(outgoing.reshape(senders, slots // senders, wide), 'alpha'...]
where the time goes in v2:
time: 24.3 us; the launch traced here: 24 us
  waiting for transfers between devices  8.78 us (36%)
  starting transfers between devices  8.4 us (35%)
  Pallas kernels  6.17 us (25%)
  other arithmetic  0.64 us (3%)
    all_to_all x1, starting transfers between devices, on_device(): lax.all_to_all(outgoing.reshape(senders, slots // senders, wide), 'alpha'...  8.32 us
    all_to_all x1, waiting for transfers between devices, on_device(): lax.all_to_all(outgoing.reshape(senders, slots // senders, wide), 'alpha'...  7.53 us
    pallas_call x1, Pallas kernels, on_device(): pl.pallas_call(lambda *refs: tables_kernel(beta_blocks, outer, inner, *re...  3.03 us
    pallas_call x1, Pallas kernels, on_device(): pl.pallas_call(lambda *refs: outgoing_kernel(strings, width, outer, inner...  1.94 us
    ppermute x1, waiting for transfers between devices, on_device(): result = result + lax.ppermute(parts[step], 'beta', route)  1.24 us
    pallas_call x1, Pallas kernels, on_device(): pl.pallas_call(lambda *refs: sigma_kernel(strings, width, *refs), out_sha...  1.2 us
    add x1, other arithmetic, on_device(): result = result + lax.ppermute(parts[step], 'beta', route)  0.64 us
  transfers between devices with their start and end apart: 2, of which 2 were waited for; matrix products, arithmetic and copies ran while one was open for 0% of the time, Pallas kernels for 13%

profile of v2, /device:TPU:0, one launch (start us, length us, event | category | flops | bytes accessed | tf_op | source)
XLA Modules:
  0.0 24.0 jit_solution(15338396108274522362)
XLA Ops:
  0.0 1.9 %outgoing.1 = (bf16[128,1024]{1,0:T(8,128)(2,1)}, s32[16,132]{1,0:T(8,128)S(1)}, s32[16,132]{1,0:T(8,128)S(1)}, s32[16,132]{1,0:T(8,128)S(1)}, s32[16,132]{1,0:T...) custom-call(bf16[64,256]{1,0:T(8,128)(2,1)} %refs_0_.1, ...), custom_call_target="tpu_custom_call" | custom-call | tf_op jit(solution)/shard_map/outgoing/pallas_call | solution.py:226
  2.0 8.3 %all-to-all-start = ((bf16[16,8,1024]{2,1,0:T(8,128)(2,1)}), bf16[16,8,1024]{2,1,0:T(8,128)(2,1)S(1)}, u32[]{:S(2)}, u32[]{:S(2)}) async-start(bf16[16,8,1024]{2,1,0:T(8,128)(2,1)} %bitcast), calls=%async_computation | async-start | bytes 524288 | tf_op jit(solution)/shard_map/all_to_all | solution.py:239
  10.3 3.0 %tables.1.refs_0_ = bf16[256,4096]{1,0:T(8,128)(2,1)S(1)} custom-call(s32[16,132]{1,0:T(8,128)S(1)} %get-tuple-element.15.refs_0_, s32[16,132]{1,0:T(8,128)S(1)} %get-tuple-element.16.refs_1_, s32[16,132]{1,0:T(8,128)S(1)} %get-tuple-element.17.refs_2_, s32[16,132]{1,0:T(8,128)S(1)} %get-tuple-element.18.refs_3_, s32[16,132]{1,0:T(8,128)S(1)} %get-tuple-element.19.refs_4_, ...), custom_call_target="tpu_custom_call" | custom-call | flops 1254899712 | bytes 8388608 | tf_op jit(solution)/shard_map/tables/pallas_call | solution.py:248
  13.3 7.5 %all-to-all-done = bf16[16,8,1024]{2,1,0:T(8,128)(2,1)S(1)} async-done(((bf16[16,8,1024]{2,1,0:T(8,128)(2,1)}), bf16[16,8,1024]{2,1,0:T(8,128)(2,1)S(1)}, u32[]{:S(2)}, u32[]{:S(2)}) %all-to-all-start) | async-done | bytes 262176 | tf_op jit(solution)/shard_map/all_to_all | solution.py:239
  20.9 1.2 %sigma.1 = (f32[64,256]{1,0:T(8,128)S(1)}, f32[64,256]{1,0:T(8,128)S(1)}) custom-call(bf16[256,4096]{1,0:T(8,128)(2,1)S(1)} %tables.1.refs_0_, bf16[128,1024]{1,0:T(8,128)(2,1)S(1)} %bitcast.2), custom_call_target="tpu_custom_call" | custom-call | tf_op jit(solution)/shard_map/sigma/pallas_call | solution.py:263
  22.1 0.1 collective-permute-start
  22.1 1.2 %collective-permute-done = f32[64,256]{1,0:T(8,128)S(1)} collective-permute-done((f32[64,256]{1,0:T(8,128)S(1)}, f32[64,256]{1,0:T(8,128)S(1)}, u32[]{:S(2)}, u32[]{:S(2)}) %collective-permute-start) | collective-permute-done | bytes 65568 | tf_op jit(solution)/shard_map/ppermute | solution.py:277
  23.4 0.6 %add.3 = f32[64,256]{1,0:T(8,128)} add(f32[64,256]{1,0:T(8,128)S(1)} %get-tuple-element.23, f32[64,256]{1,0:T(8,128)S(1)} %collective-permute-done) | non-fusion elementwise | flops 16384 | bytes 196608 | tf_op jit(solution)/shard_map/add | solution.py:277
Async XLA Ops:
  2.0 18.9 %all-to-all-start = ((bf16[16,8,1024]{2,1,0:T(8,128)(2,1)}), bf16[16,8,1024]{2,1,0:T(8,128)(2,1)S(1)}, u32[]{:S(2)}, u32[]{:S(2)}) async-start(bf16[16,8,1024]{2,1,0:T(8,128)(2,1)} %bitcast), calls=%async_computation | async-start | bytes 524288 | tf_op jit(solution)/shard_map/all_to_all | solution.py:239
  22.1 1.3 %collective-permute-start = (f32[64,256]{1,0:T(8,128)S(1)}, f32[64,256]{1,0:T(8,128)S(1)}, u32[]{:S(2)}, u32[]{:S(2)}) collective-permute-start(f32[64,256]{1,0:T(8,128)S(1)} %get-tuple-element.24), channel_id=1, source_target_pairs={{0,1},{1,0},{2,3},{3,2},{4,5},{5,4},{6,7},{7,6},{8,9},{9,8},{10,11... | collective-permute-start | bytes 196616 | tf_op jit(solution)/shard_map/ppermute | solution.py:277
